TPU v7x, 32 devices: a whole 2x2x4 slice. The times are simulated.
32 devices in a mesh: shot: 8 (over z, core), brick: 4 (over y, x).
Axes of the slice: x: 2, y: 2, z: 4, core: 2. Of those that a mesh axis runs over, the one named last changes fastest.
Arguments:
- sources: float32 [8, 2, 2, 256, 32, 256], P('shot', None, None, None, 'brick'), may hold values from -24 to 24
- slowness: float32 [8, 256, 32, 256], P('shot', None, 'brick'), may hold values from 0.5 to 2
- group_size: int32 [8], replicated, may hold values from 2 to 4, as said below
- window_anchor: int32 [8], replicated, may hold values from 0 to 24
- tile_slot: int32 [32], replicated, may hold values from 0 to 31, each once
Outputs:
- gradient: float32 [4, 32, 65536], P('brick', 'shot')
Inputs may be any that keep to these rules, and one draw needn't show every extreme that they name: `group_size`: some shot spans all 4 bricks and some shot only 2. Window s covers model tiles window_anchor[s] to window_anchor[s] + 7. `tile_slot`: each slot of 0 to 31 once.
All inputs are finite; a program needn't handle non-finite values.
Results may differ from a plain program's by a relative error of at most 0.0003.
Values sent between devices are 32-bit elements; how exact they have to be, the bound alone decides.
A program may use at most 128 MiB of HBM per device.

v0:
```python
import jax
import jax.numpy as jnp
from jax import lax
from jax.sharding import PartitionSpec as P

BLOCKS = 8


shift_beta = 0.5
relaxation = 0.8


def extended(value, sides, width):
    for axis, dim in sides:
        size, length = (lax.axis_size(axis), value.shape[dim])
        up = [(i, (i + 1) % size) for i in range(size - 1)]
        down = [(j, i) for i, j in up]
        last = lax.slice_in_dim(value, length - width, length, axis=dim)
        first = lax.slice_in_dim(value, 0, width, axis=dim)
        before = lax.ppermute(last, axis, up)
        after = lax.ppermute(first, axis, down)
        value = jnp.concatenate([before, value, after], axis=dim)
    return value


def lateral_sum(field):
    summed = jnp.zeros_like(field)
    for along_axis in (1, 3):
        widths = [(0, 0)] * 4
        widths[along_axis] = (1, 1)
        padded = jnp.pad(field, widths)
        count = field.shape[along_axis]
        summed = summed + lax.slice_in_dim(padded, 0, count, axis=along_axis)
        summed = summed + lax.slice_in_dim(padded, 2, count + 2, axis=along_axis)
    return summed


def apply_inverse(values, inv_re, inv_im):
    fwd_re = values[0] * inv_re - values[1] * inv_im
    fwd_im = values[0] * inv_im + values[1] * inv_re
    adj_re = values[2] * inv_re - values[3] * inv_im
    adj_im = values[2] * inv_im + values[3] * inv_re
    return jnp.stack([fwd_re, fwd_im, adj_re, adj_im])


def sine_taper(count, extent):
    positions = jnp.arange(count, dtype=jnp.int32).astype(jnp.float32)
    return jnp.sin(jnp.pi * (positions + 0.5) / extent)


def per_device(sources, slowness, group_size, window_anchor, tile_slot):
    slowness_window = slowness[0]
    wide_y, planes, wide_z = slowness_window.shape
    brick_index = lax.axis_index("brick")
    shot_index = lax.axis_index("shot")
    extent = group_size[shot_index] * planes
    depth_ids = brick_index * planes + jnp.arange(planes, dtype=jnp.int32)
    active = depth_ids < extent
    active_mask = active.astype(jnp.float32)[None, :, None]
    real_d = 6.0 - slowness_window
    imag_d = shift_beta * slowness_window
    denominator = real_d * real_d + imag_d * imag_d
    inv_re = real_d / denominator
    inv_im = imag_d / denominator
    forcing = sources[0].reshape(4, wide_y, planes, wide_z)
    field = relaxation * apply_inverse(forcing, inv_re, inv_im) * active_mask
    padded = extended(field, (("brick", 2),), 1)
    neighbours = padded[:, :, :-2, :] + padded[:, :, 2:, :] + lateral_sum(field)
    updated = apply_inverse(forcing + neighbours, inv_re, inv_im)
    field = ((1.0 - relaxation) * field + relaxation * updated) * active_mask
    imaging = (
        field[0] * field[2]
        - field[1] * field[3]
        - shift_beta * (field[0] * field[3] + field[1] * field[2])
    )
    extent_float = extent.astype(jnp.float32)
    depth_float = depth_ids.astype(jnp.float32)
    taper_x = jnp.where(active, jnp.sin(jnp.pi * (depth_float + 0.5) / extent_float), 0.0)
    taper_y = sine_taper(wide_y, float(wide_y))
    taper_z = sine_taper(wide_z, float(wide_z))
    gradient = imaging * (taper_y[:, None, None] * taper_x[None, :, None] * taper_z[None, None, :])
    blocks = gradient.reshape(BLOCKS, -1)
    shot_count = lax.axis_size("shot")
    tile_dev = tile_slot.shape[0] // shot_count
    owned = shot_index * tile_dev + jnp.arange(tile_dev, dtype=jnp.int32)
    piece_slots = tile_slot[window_anchor[:, None] + jnp.arange(BLOCKS, dtype=jnp.int32)[None, :]]
    weights = (owned[:, None, None] == piece_slots[None, :, :]).astype(jnp.float32)
    summed = jnp.einsum(
        "qkb,kbc->qc",
        weights,
        lax.all_gather(blocks[None], "shot", axis=0, tiled=True),
        precision=lax.Precision.HIGHEST,
    )
    return summed[None]


def solution(mesh):
    return jax.shard_map(
        per_device,
        mesh=mesh,
        in_specs=(
            P("shot", None, None, None, "brick", None),
            P("shot", None, "brick", None),
            P(),
            P(),
            P(),
        ),
        out_specs=P("brick", "shot", None),
        check_vma=False,
    )
```

profile of v0, /device:TPU:0, one launch (start us, length us, event | category | flops | bytes accessed | tf_op | source)
XLA Modules:
  0.0 299.8 jit_solution(18021626518816931088)
XLA Ops:
  6.5 0.0 copy-start
  6.5 0.0 all-gather.2.cloned.1.call-start
  6.5 1.2 dynamic_slice.3
  8.4 0.0 copy-start.9
  8.5 6.1 %copy.14 = f32[1,2,2,256,8,256]{5,3,4,2,1,0:T(8,128)S(1)} copy(f32[1,2,2,256,8,256]{5,4,3,2,1,0:T(8,128)} %param.5) | data formatting | bytes 16777216 | tf_op args[0]
  14.6 0.0 copy-start.1
  14.6 0.1 sine_select_fusion
  14.6 0.0 copy-done.9
  14.6 2.0 multiply_subtract_fusion.4
  16.6 1.2 copy-done.1
  17.8 0.0 copy-start.3
  17.8 0.0 copy-start.5
  17.8 0.0 copy-start.7
  17.8 1.0 maximum_multiply_fusion
  18.8 0.4 copy-done.3
  19.2 0.6 copy-done.5
  19.8 0.6 copy-done.7
  20.4 0.0 copy-start.2
  20.4 3.2 %copy-done.2 = f32[4,256,8,256]{3,1,2,0:T(8,128)} copy-done((f32[4,256,8,256]{3,1,2,0:T(8,128)}, f32[4,256,8,256]{3,1,2,0:T(8,128)S(1)}, u32[]{:S(2)}) %copy-start.2) | copy-done | bytes 8388632
  23.6 1.2 fusion.15
  24.8 5.8 %collective-permute-start = (f32[4,256,1,256]{3,1,2,0:T(8,128)}, f32[4,256,1,256]{3,1,2,0:T(8,128)}, u32[]{:S(2)}, u32[]{:S(2)}) collective-permute-start(f32[4,256,1,256]{3,1,2,0:T(8,128)} %get-tuple-element.13), channel_id=1, source_target_pairs={{0,1},{1,2},{2,3},{4,5},{5,6},{6,7},{8,9},{9,10},{10,11},{12,13},{... | collective-permute-start | bytes 3145736 | tf_op jit(solution)/shard_map/ppermute | solution.py:20
  30.6 1.3 collective-permute-start.1
  32.0 0.1 broadcast_multiply_fusion.1
  32.1 1.7 broadcast_multiply_fusion
  33.8 3.3 %mul.300 = f32[1,8,65536]{2,1,0:T(8,128)} reshape(f32[256,8,256]{2,1,0:T(8,128)} %broadcast_multiply_fusion) | data formatting | bytes 4194304 | tf_op jit(solution)/shard_map/mul | solution.py:81
  37.1 0.0 copy-start.10
  37.1 15.2 %collective-permute-done = f32[4,256,1,256]{3,1,2,0:T(8,128)} collective-permute-done((f32[4,256,1,256]{3,1,2,0:T(8,128)}, f32[4,256,1,256]{3,1,2,0:T(8,128)}, u32[]{:S(2)}, u32[]{:S(2)}) %collective-permute-start) | collective-permute-done | bytes 1048608 | tf_op jit(solution)/shard_map/ppermute | solution.py:20
  52.4 24.4 %collective-permute-done.1 = f32[4,256,1,256]{3,1,2,0:T(8,128)} collective-permute-done((f32[4,256,1,256]{3,1,2,0:T(8,128)S(1)}, f32[4,256,1,256]{3,1,2,0:T(8,128)}, u32[]{:S(2)}, u32[]{:S(2)}) %collective-permute-start.1) | collective-permute-done | bytes 1048608 | tf_op jit(solution)/shard_map/ppermute | solution.py:21
  76.8 23.1 %fusion.4 = f32[4,256,8,256]{3,1,2,0:T(8,128)S(1)} fusion(f32[4,256,8,256]{3,1,2,0:T(8,128)} %copy-done.2, f32[4,256,1,256]{3,1,2,0:T(8,128)} %collective-permute-done.1, f32[4,256,1,256]{3,1,2,0:T(8,128)} %collective-permute-done, f32[1,2,2,256,8,256]{5,3,4,2,1,0:T(8,128)} %copy-done.1), kind=kLoop, calls=%fused_computation.8 | loop fusion | flops 16777216 | bytes 27262976 | tf_op jit(solution)/shard_map/add | solution.py:69
  99.9 0.0 copy-done.10
  99.9 0.0 copy-start.4
  99.9 0.0 copy-start.6
  99.9 0.0 copy-start.8
  99.9 3.9 %multiply_subtract_fusion.2 = (f32[1,256,8,256]{3,1,2,0:T(8,128)S(1)}, f32[1,256,8,256]{3,1,2,0:T(8,128)}, f32[1,256,8,256]{3,1,2,0:T(8,128)}, f32[1,256,8,256]{3,1,2,0:T(8,128)}) fusion(f32[4,256,8,256]{3,1,2,0:T(8,128)S(1)} %fusion.4, f32[1,256,8,256]{3,2,1,0:T(8,128)S(1)} %copy-done.10), kind=kLoop, calls=%fused_computation.20 | loop fusion | flops 9961472 | bytes 18874368 | tf_op jit(solution)/shard_map/sub | solution.py:39
  103.9 0.0 copy-done.4
  103.9 0.0 copy-done.6
  103.9 1.1 copy-done.8
  105.0 4.2 %fusion.7 = f32[4,256,8,256]{3,1,2,0:T(8,128)S(1)} fusion(f32[1,256,8,256]{3,1,2,0:T(8,128)} %get-tuple-element.7, f32[1,256,8,256]{3,1,2,0:T(8,128)} %get-tuple-element.6, f32[1,256,8,256]{3,1,2,0:T(8,128)} %get-tuple-element.8, f32[1,256,8,256]{3,1,2,0:T(8,128)S(1)} %get-tuple-element.5, f32[8]{0:T(128)S(1)} %fusion.14, f32[8]{0:T(128)S(1)} %get-tuple-element.16, ...), kind=kLoop, calls=%fused_computation.15 | loop fusion | flops 23068672 | bytes 25165888 | tf_op jit(solution)/shard_map/mul | solution.py:70
  109.2 0.6 multiply_subtract_fusion
  109.8 2.5 copy.17
  112.3 0.0 copy-start.11
  112.3 3.4 %sub.62 = f32[1,8,65536]{2,1,0:T(8,128)} reshape(f32[1,256,8,256]{3,2,1,0:T(8,128)} %copy.17) | data formatting | bytes 4194304 | tf_op jit(solution)/shard_map/sub | solution.py:72
  115.7 0.0 copy-done.11
  115.7 3.3 %mul.301 = f32[1,8,65536]{2,1,0:T(8,128)} multiply(f32[1,8,65536]{2,1,0:T(8,128)} %sub.62, f32[1,8,65536]{2,1,0:T(8,128)S(1)} %copy-done.11) | non-fusion elementwise | flops 524288 | bytes 6291456 | tf_op jit(solution)/shard_map/mul | solution.py:81
  119.0 0.0 copy-start.12
  119.0 0.0 all-gather.2.cloned.1.call-update
  119.0 0.6 copy-done.12
  119.7 0.1 compare_select_fusion
  119.7 0.1 reshape.222
  119.8 0.0 copy-done
  119.8 0.8 gather_fusion
  120.6 0.1 reshape.221
  120.7 0.1 copy.13
  120.8 149.8 %all-gather.2.cloned.1.call-done = f32[8,8,65536]{2,1,0:T(8,128)} async-done(((f32[1,8,65536]{2,1,0:T(8,128)}), f32[8,8,65536]{2,1,0:T(8,128)}) %all-gather.2.cloned.1.call-update) | async-done | bytes 16777232 | tf_op jit(solution)/shard_map/all_gather | solution.py:91
  270.6 22.3 %convolution_bitcast_fusion = f32[1,4,65536]{2,1,0:T(4,128)} fusion(f32[8,8,65536]{2,1,0:T(8,128)} %all-gather.2.cloned.1.call-done, s32[8,8]{0,1:T(8,128)S(1)} %copy.13, s32[4]{0:T(128)S(1)} %iota_add_fusion.1), kind=kOutput, calls=%fused_computation.1 | convolution fusion | flops 201326848 | bytes 17826064 | tf_op jit(solution)/shard_map/qkb,kbc->qc/dot_general | solution.py:88
  (4 shorter events, 0.1 us)
Async XLA Ops:
  6.5 113.3 %copy-start = (s32[32]{0:T(128)S(1)}, s32[32]{0:T(128)}, u32[]{:S(2)}) copy-start(s32[32]{0:T(128)} %param.9) | copy-start | bytes 388
  6.5 264.1 %all-gather.2.cloned.1.call-start = ((), (), s32[]{:S(2)}) async-start(), calls=%async_computation | async-start | bytes 18874368 | tf_op jit(solution)/shard_map/all_gather | solution.py:91
  8.4 6.2 %copy-start.9 = (f32[1,256,8,256]{3,2,1,0:T(8,128)S(1)}, f32[1,256,8,256]{3,2,1,0:T(8,128)}, u32[]{:S(2)}) copy-start(f32[1,256,8,256]{3,2,1,0:T(8,128)} %param.6) | copy-start | bytes 6291460
  14.6 3.2 %copy-start.1 = (f32[1,2,2,256,8,256]{5,3,4,2,1,0:T(8,128)}, f32[1,2,2,256,8,256]{5,3,4,2,1,0:T(8,128)S(1)}, u32[]{:S(2)}) copy-start(f32[1,2,2,256,8,256]{5,3,4,2,1,0:T(8,128)S(1)} %copy.14) | copy-start | bytes 25165828
  17.8 1.4 copy-start.3
  17.8 2.0 copy-start.5
  17.8 2.6 copy-start.7
  20.4 3.2 %copy-start.2 = (f32[4,256,8,256]{3,1,2,0:T(8,128)}, f32[4,256,8,256]{3,1,2,0:T(8,128)S(1)}, u32[]{:S(2)}) copy-start(f32[4,256,8,256]{3,1,2,0:T(8,128)S(1)} %maximum_multiply_fusion) | copy-start | bytes 25165828
  24.8 27.6 %collective-permute-start = (f32[4,256,1,256]{3,1,2,0:T(8,128)}, f32[4,256,1,256]{3,1,2,0:T(8,128)}, u32[]{:S(2)}, u32[]{:S(2)}) collective-permute-start(f32[4,256,1,256]{3,1,2,0:T(8,128)} %get-tuple-element.13), channel_id=1, source_target_pairs={{0,1},{1,2},{2,3},{4,5},{5,6},{6,7},{8,9},{9,10},{10,11},{12,13},{... | collective-permute-start | bytes 3145736 | tf_op jit(solution)/shard_map/ppermute | solution.py:20
  30.6 46.1 %collective-permute-start.1 = (f32[4,256,1,256]{3,1,2,0:T(8,128)S(1)}, f32[4,256,1,256]{3,1,2,0:T(8,128)}, u32[]{:S(2)}, u32[]{:S(2)}) collective-permute-start(f32[4,256,1,256]{3,1,2,0:T(8,128)S(1)} %get-tuple-element.14), channel_id=1, source_target_pairs={{1,0},{2,1},{3,2},{5,4},{6,5},{7,6},{9,8},{10,9},{11,10},{13,12},{... | collective-permute-start | bytes 3145736 | tf_op jit(solution)/shard_map/ppermute | solution.py:21
  37.1 62.8 %copy-start.10 = (f32[1,256,8,256]{3,2,1,0:T(8,128)S(1)}, f32[1,256,8,256]{3,2,1,0:T(8,128)}, u32[]{:S(2)}) copy-start(f32[1,256,8,256]{3,2,1,0:T(8,128)} %param.6) | copy-start | bytes 6291460
  99.9 4.0 %copy-start.4 = (f32[1,256,8,256]{3,1,2,0:T(8,128)S(1)}, f32[1,256,8,256]{3,1,2,0:T(8,128)}, u32[]{:S(2)}) copy-start(f32[1,256,8,256]{3,1,2,0:T(8,128)} %copy-done.3) | copy-start | bytes 6291460
  99.9 4.0 %copy-start.6 = (f32[1,256,8,256]{3,1,2,0:T(8,128)S(1)}, f32[1,256,8,256]{3,1,2,0:T(8,128)}, u32[]{:S(2)}) copy-start(f32[1,256,8,256]{3,1,2,0:T(8,128)} %copy-done.5) | copy-start | bytes 6291460
  99.9 5.1 %copy-start.8 = (f32[1,256,8,256]{3,1,2,0:T(8,128)S(1)}, f32[1,256,8,256]{3,1,2,0:T(8,128)}, u32[]{:S(2)}) copy-start(f32[1,256,8,256]{3,1,2,0:T(8,128)} %copy-done.7) | copy-start | bytes 6291460
  112.3 3.4 %copy-start.11 = (f32[1,8,65536]{2,1,0:T(8,128)S(1)}, f32[1,8,65536]{2,1,0:T(8,128)}, u32[]{:S(2)}) copy-start(f32[1,8,65536]{2,1,0:T(8,128)} %mul.300) | copy-start | bytes 6291460
  119.0 0.7 copy-start.12
Sparse Core Ops, SparseCore 0:
  119.2 151.3 all-gather.1
where the time goes:
time: 300 us
  waiting for transfers between devices  189 us (63%)
  other arithmetic  40.1 us (13%)
  local copies, waits for them, and re-layouts  26.6 us (9%)
  matrix products  22.3 us (7%)
  between operations  14.2 us (5%)
  starting transfers between devices  7.11 us (2%)
    all_gather x1, waiting for transfers between devices, per_device(): lax.all_gather(blocks[None], 'shot', axis=0, tiled=True)  150 us
    ppermute x1, waiting for transfers between devices, extended(): after = lax.ppermute(first, axis, down)  24.4 us
    add x1, other arithmetic, per_device(): updated = apply_inverse(forcing + neighbours, inv_re, inv_im)  23.1 us
    dot_general x1, matrix products, per_device(): jnp.einsum('qkb,kbc->qc', weights, lax.all_gather(blocks[None], 'shot', a...  22.3 us
    ppermute x1, waiting for transfers between devices, extended(): before = lax.ppermute(last, axis, up)  15.2 us
    unnamed x27, local copies, waits for them, and re-layouts  13.9 us
  transfers between devices with their start and end apart: 3, of which 3 were waited for; matrix products, arithmetic and copies ran while one was open for 2% of the time, Pallas kernels for 0%

commit v1 on v0

v1 whole, which is shorter than its diff:
```python
import functools

import jax
import jax.numpy as jnp
from jax import lax
from jax.experimental import pallas as pl
from jax.experimental.pallas import tpu as pltpu
from jax.sharding import PartitionSpec as P

BLOCKS = 8
ROWS = 2
MESH = pl.DeviceIdType.MESH

shift_beta = 0.5
relaxation = 0.8


def kernel(
    shots, bricks, per_dev, chunks,
    mask_ref, ty_ref, wt_ref, txz_ref, src_ref, slow_ref,
    out_ref,
    sbuf, wbuf, f1, inv, hs_up, hs_dn, h_before, h_after, gsend, raw,
    rin, rout, lin, lout, own, fin,
    in_sem, win_sem, up_s, up_r, dn_s, dn_r, sib_s, sib_r, rt_s, rt_r, lt_s, lt_r, fin_s, fin_r,
):
    shot = lax.axis_index("shot")
    brick = lax.axis_index("brick")
    pair, core = shot // 2, shot % 2
    sib = pair * 2 + (1 - core)
    pairs = shots // 2
    group = 2 * per_dev
    both = 2 * BLOCKS
    half_rows = chunks * ROWS
    wide_y = 2 * BLOCKS * half_rows

    def source_copies(k, slot):
        return (
            pltpu.make_async_copy(src_ref.at[:, :, k], sbuf.at[slot], in_sem.at[slot]),
            pltpu.make_async_copy(slow_ref.at[:, k], wbuf.at[slot], win_sem.at[slot]),
        )

    for copy in source_copies(0, 0):
        copy.start()

    barrier = pltpu.get_barrier_semaphore()

    def greet(s, b):
        pl.semaphore_signal(barrier, inc=1, device_id=(s, b), device_id_type=MESH)

    greet(sib, brick)

    @pl.when(brick > 0)
    def _():
        greet(shot, brick - 1)

    @pl.when(brick < bricks - 1)
    def _():
        greet(shot, brick + 1)

    @pl.when(pair > 0)
    def _():
        greet(shot - 2, brick)

    @pl.when(pair < pairs - 1)
    def _():
        greet(shot + 2, brick)

    @pl.when(brick == 0)
    def _():
        h_before[...] = jnp.zeros_like(h_before)

    @pl.when(brick == bricks - 1)
    def _():
        h_after[...] = jnp.zeros_like(h_after)

    zero_row = jnp.zeros((1,) + f1.shape[2:], jnp.float32)
    for c in range(4):
        f1[c, pl.ds(0, 1)] = zero_row
        f1[c, pl.ds(wide_y + 1, 1)] = zero_row

    one = jnp.int32(1)
    nothing = jnp.int32(0)
    friends = (
        one
        + jnp.where(brick > 0, one, nothing)
        + jnp.where(brick < bricks - 1, one, nothing)
        + jnp.where(pair > 0, one, nothing)
        + jnp.where(pair < pairs - 1, one, nothing)
    )
    pl.semaphore_wait(barrier, friends)

    def up_copy(k):
        return pltpu.make_async_remote_copy(
            src_ref=hs_up.at[k], dst_ref=h_before.at[k], send_sem=up_s.at[k], recv_sem=up_r.at[k],
            device_id=(shot, brick + 1), device_id_type=MESH)

    def dn_copy(k):
        return pltpu.make_async_remote_copy(
            src_ref=hs_dn.at[k], dst_ref=h_after.at[k], send_sem=dn_s.at[k], recv_sem=dn_r.at[k],
            device_id=(shot, brick - 1), device_id_type=MESH)

    mask = mask_ref[0]

    def first(k, carry):
        slot = lax.rem(k, 2)

        @pl.when(k + 1 < chunks)
        def _():
            for copy in source_copies(k + 1, 1 - slot):
                copy.start()

        for copy in source_copies(k, slot):
            copy.wait()

        def rows(j, carry):
            y = j * half_rows + k * ROWS
            w = wbuf[slot, j]
            real_d = 6.0 - w
            imag_d = shift_beta * w
            scale = relaxation / (real_d * real_d + imag_d * imag_d)
            ire = real_d * scale
            iim = imag_d * scale
            inv[0, pl.ds(y, ROWS)] = ire
            inv[1, pl.ds(y, ROWS)] = iim
            mre, mim = ire * mask, iim * mask
            for p in range(2):
                a, b = sbuf[slot, 2 * p, j], sbuf[slot, 2 * p + 1, j]
                fre = a * mre - b * mim
                fim = a * mim + b * mre
                for c, f in ((2 * p, fre), (2 * p + 1, fim)):
                    f1[c, pl.ds(y + 1, ROWS)] = f
                    for r in range(ROWS):
                        hs_dn[k, c, pl.ds(j * ROWS + r, 1), :] = f[r, 0:1, :]
                        hs_up[k, c, pl.ds(j * ROWS + r, 1), :] = f[r, 7:8, :]
            return carry

        lax.fori_loop(0, both, rows, 0)

        @pl.when(brick < bricks - 1)
        def _():
            up_copy(k).start()

        @pl.when(brick > 0)
        def _():
            dn_copy(k).start()

        return carry

    lax.fori_loop(0, chunks, first, 0)

    planes, wide_z = f1.shape[2:]
    lane = lax.broadcasted_iota(jnp.int32, (planes, wide_z), 1)
    sub = lax.broadcasted_iota(jnp.int32, (planes, wide_z), 0)

    def image(k, j, r):
        y = j * half_rows + k * ROWS + r
        hrow = j * ROWS + r
        centre, near = [], []
        for c in range(4):
            f = f1[c, y + 1]
            total = f1[c, y] + f1[c, y + 2]
            total += jnp.where(lane == 0, 0.0, pltpu.roll(f, 1, axis=1))
            total += jnp.where(lane == wide_z - 1, 0.0, pltpu.roll(f, wide_z - 1, axis=1))
            total += jnp.where(sub == 0, h_before[k, c, pl.ds(hrow, 1), :], pltpu.roll(f, 1, axis=0))
            total += jnp.where(sub == planes - 1, h_after[k, c, pl.ds(hrow, 1), :], pltpu.roll(f, planes - 1, axis=0))
            centre.append(f)
            near.append(total)
        ire, iim = inv[0, y], inv[1, y]
        keep = 2.0 - relaxation
        field = []
        for p in (0, 2):
            field.append(keep * centre[p] + (near[p] * ire - near[p + 1] * iim))
            field.append(keep * centre[p + 1] + (near[p] * iim + near[p + 1] * ire))
        imaging = (
            field[0] * field[2]
            - field[1] * field[3]
            - shift_beta * (field[0] * field[3] + field[1] * field[2])
        )
        return imaging * (txz_ref[...] * ty_ref[y])

    def sib_copy(k):
        return pltpu.make_async_remote_copy(
            src_ref=gsend.at[k], dst_ref=raw.at[k, pl.ds(core * BLOCKS, BLOCKS)],
            send_sem=sib_s.at[k], recv_sem=sib_r.at[k],
            device_id=(sib, brick), device_id_type=MESH)

    def sib_wait(k):
        pltpu.make_async_remote_copy(
            src_ref=gsend.at[k], dst_ref=raw.at[k, pl.ds((1 - core) * BLOCKS, BLOCKS)],
            send_sem=sib_s.at[k], recv_sem=sib_r.at[k],
            device_id=(sib, brick), device_id_type=MESH).wait_recv()

    def right_copy(k, s):
        count = both if s == 0 else (pairs - 1 - s) * group
        return pltpu.make_async_remote_copy(
            src_ref=raw.at[k] if s == 0 else rout.at[k, pl.ds(0, count)],
            dst_ref=rin.at[k, pl.ds(0, count)],
            send_sem=rt_s.at[k], recv_sem=rt_r.at[k],
            device_id=(2 * (s + 1) + core, brick), device_id_type=MESH)

    def left_copy(k, s):
        count = both if s == pairs - 1 else s * group
        return pltpu.make_async_remote_copy(
            src_ref=raw.at[k] if s == pairs - 1 else lout.at[k, pl.ds(0, count)],
            dst_ref=lin.at[k, pl.ds(0, count)],
            send_sem=lt_s.at[k], recv_sem=lt_r.at[k],
            device_id=(2 * (s - 1) + core, brick), device_id_type=MESH)

    def fin_copy(k):
        return pltpu.make_async_remote_copy(
            src_ref=own.at[k, pl.ds((1 - core) * per_dev, per_dev)], dst_ref=fin.at[k],
            send_sem=fin_s.at[k], recv_sem=fin_r.at[k],
            device_id=(sib, brick), device_id_type=MESH)

    def weighted(buf, k, r, source_pair):
        start = (r * shots + 2 * source_pair) * BLOCKS
        total = wt_ref[start] * buf[k, 0]
        for q in range(1, both):
            total += wt_ref[start + q] * buf[k, q]
        return total

    def produce(k):
        @pl.when(brick > 0)
        def _():
            pltpu.make_async_remote_copy(
                src_ref=hs_up.at[k], dst_ref=h_before.at[k], send_sem=up_s.at[k], recv_sem=up_r.at[k],
                device_id=(shot, brick - 1), device_id_type=MESH).wait_recv()

        @pl.when(brick < bricks - 1)
        def _():
            pltpu.make_async_remote_copy(
                src_ref=hs_dn.at[k], dst_ref=h_after.at[k], send_sem=dn_s.at[k], recv_sem=dn_r.at[k],
                device_id=(shot, brick + 1), device_id_type=MESH).wait_recv()

        def other(b, carry):
            for r in range(ROWS):
                gsend[k, b, r] = image(k, 2 * b + (1 - core), r)
            return carry

        lax.fori_loop(0, BLOCKS, other, 0)
        sib_copy(k).start()

        def mine(b, carry):
            for r in range(ROWS):
                raw[k, core * BLOCKS + b, r] = image(k, 2 * b + core, r)
            return carry

        lax.fori_loop(0, BLOCKS, mine, 0)

    def right_flow(k):
        for s in range(pairs - 1):
            @pl.when(pair == s + 1)
            def _(s=s):
                right_copy(k, s).wait_recv()

        for s in range(pairs - 1):
            @pl.when(pair == s)
            def _(s=s):
                if s > 0:
                    def body(q, carry):
                        r = (s + 1) * group + q
                        total = weighted(raw, k, r, s)
                        if s == 1:
                            total += weighted(rin, k, r, 0)
                        else:
                            total += rin[k, q + group]
                        rout[k, q] = total
                        return carry

                    lax.fori_loop(0, (pairs - 1 - s) * group, body, 0)
                right_copy(k, s).start()

    def left_flow(k):
        for s in range(1, pairs):
            @pl.when(pair == s - 1)
            def _(s=s):
                left_copy(k, s).wait_recv()

        for s in range(1, pairs):
            @pl.when(pair == s)
            def _(s=s):
                if s < pairs - 1:
                    def body(q, carry):
                        total = weighted(raw, k, q, s)
                        if s == pairs - 2:
                            total += weighted(lin, k, q, pairs - 1)
                        else:
                            total += lin[k, q]
                        lout[k, q] = total
                        return carry

                    lax.fori_loop(0, s * group, body, 0)
                left_copy(k, s).start()

    def finish(k):
        for s in range(pairs):
            @pl.when(pair == s)
            def _(s=s):
                def body(q, carry):
                    r = s * group + q
                    total = weighted(raw, k, r, s)
                    if s == 1:
                        total += weighted(rin, k, r, 0)
                    elif s > 1:
                        total += rin[k, q]
                    if s == pairs - 2:
                        total += weighted(lin, k, r, pairs - 1)
                    elif s < pairs - 1:
                        total += lin[k, s * group + q]
                    own[k, q] = total
                    return carry

                lax.fori_loop(0, group, body, 0)

        fin_copy(k).start()
        for q in range(per_dev):
            out_ref[q, core, k] = own[k, core * per_dev + q]

    near_lag, far_lag, end_lag = 1, 2, 3
    is_left = pair < pairs // 2
    right_lag = jnp.where(is_left, near_lag, far_lag)
    left_lag = jnp.where(is_left, far_lag, near_lag)

    def step(t, carry):
        @pl.when(t < chunks)
        def _():
            produce(t)

        @pl.when((t >= 1) & (t < chunks + 1))
        def _():
            sib_wait(t - 1)

        kr = t - right_lag
        kl = t - left_lag

        @pl.when((kr >= 0) & (kr < chunks))
        def _():
            right_flow(kr)

        @pl.when((kl >= 0) & (kl < chunks))
        def _():
            left_flow(kl)

        @pl.when(t >= end_lag)
        def _():
            finish(t - end_lag)

        return carry

    lax.fori_loop(0, chunks + end_lag, step, 0)

    def drain(k, carry):
        fin_copy(k).wait_recv()
        for q in range(per_dev):
            out_ref[q, 1 - core, k] = fin[k, q]
        fin_copy(k).wait_send()
        sib_copy(k).wait_send()

        @pl.when(brick < bricks - 1)
        def _():
            up_copy(k).wait_send()

        @pl.when(brick > 0)
        def _():
            dn_copy(k).wait_send()

        for s in range(pairs - 1):
            @pl.when(pair == s)
            def _(s=s):
                right_copy(k, s).wait_send()

            @pl.when(pair == s + 1)
            def _(s=s):
                left_copy(k, s + 1).wait_send()

        return carry

    lax.fori_loop(0, chunks, drain, 0)


def sine_taper(count, extent):
    positions = jnp.arange(count, dtype=jnp.int32).astype(jnp.float32)
    return jnp.sin(jnp.pi * (positions + 0.5) / extent)


def per_device(shots, bricks, sources, slowness, group_size, window_anchor, tile_slot):
    wide_y, planes, wide_z = slowness.shape[1:]
    half_rows = wide_y // (2 * BLOCKS)
    chunks = half_rows // ROWS
    brick_index = lax.axis_index("brick")
    shot_index = lax.axis_index("shot")
    tiles = tile_slot.shape[0]
    per_dev = tiles // shots
    pairs = shots // 2
    group = 2 * per_dev
    both = 2 * BLOCKS

    extent = group_size[shot_index] * planes
    depth_ids = brick_index * planes + jnp.arange(planes, dtype=jnp.int32)
    active = depth_ids < extent
    mask = (brick_index < group_size[shot_index]).astype(jnp.float32).reshape(1)
    taper_x = jnp.where(
        active,
        jnp.sin(jnp.pi * (depth_ids.astype(jnp.float32) + 0.5) / extent.astype(jnp.float32)),
        0.0,
    )
    taper_xz = taper_x[:, None] * sine_taper(wide_z, float(wide_z))[None, :]
    taper_y = sine_taper(wide_y, float(wide_y))
    piece_slots = tile_slot[window_anchor[:, None] + jnp.arange(BLOCKS, dtype=jnp.int32)[None, :]]
    slots = jnp.arange(tiles, dtype=jnp.int32)
    weights = (slots[:, None, None] == piece_slots[None]).astype(jnp.float32).reshape(-1)

    chunk = (ROWS, planes, wide_z)
    src = sources.reshape((4, 2 * BLOCKS, chunks) + chunk)
    slow = slowness.reshape((2 * BLOCKS, chunks) + chunk)
    f32 = jnp.float32
    wide = max(both, (pairs - 2) * group)
    fwd = max(group, (pairs - 2) * group)
    dma = pltpu.SemaphoreType.DMA
    smem = pl.BlockSpec(memory_space=pltpu.SMEM)
    vmem = pl.BlockSpec(memory_space=pltpu.VMEM)
    hbm = pl.BlockSpec(memory_space=pl.ANY)
    halo = pltpu.VMEM((chunks, 4, both * ROWS, wide_z), f32)
    out = pl.pallas_call(
        functools.partial(kernel, shots, bricks, per_dev, chunks),
        out_shape=jax.ShapeDtypeStruct((per_dev, 2, chunks) + chunk, f32),
        in_specs=[smem, smem, smem, vmem, hbm, hbm],
        out_specs=vmem,
        scratch_shapes=[
            pltpu.VMEM((2, 4, both) + chunk, f32),
            pltpu.VMEM((2, both) + chunk, f32),
            pltpu.VMEM((4, wide_y + 2, planes, wide_z), f32),
            pltpu.VMEM((2, wide_y, planes, wide_z), f32),
            halo, halo, halo, halo,
            pltpu.VMEM((chunks, BLOCKS) + chunk, f32),
            pltpu.VMEM((chunks, both) + chunk, f32),
            pltpu.VMEM((chunks, wide) + chunk, f32),
            pltpu.VMEM((chunks, fwd) + chunk, f32),
            pltpu.VMEM((chunks, wide) + chunk, f32),
            pltpu.VMEM((chunks, fwd) + chunk, f32),
            pltpu.VMEM((chunks, group) + chunk, f32),
            pltpu.VMEM((chunks, per_dev) + chunk, f32),
            dma((2,)), dma((2,)),
        ] + [dma((chunks,))] * 12,
        compiler_params=pltpu.CompilerParams(
            collective_id=0, has_side_effects=True, vmem_limit_bytes=62 * 1024 * 1024
        ),
        cost_estimate=pl.CostEstimate(
            flops=200 * wide_y * planes * wide_z, bytes_accessed=12 * 1024 * 1024, transcendentals=0
        ),
    )(mask, taper_y, weights, taper_xz, src, slow)
    return out.reshape(1, per_dev, -1)


def solution(mesh):
    return jax.shard_map(
        functools.partial(per_device, mesh.shape["shot"], mesh.shape["brick"]),
        mesh=mesh,
        in_specs=(
            P("shot", None, None, None, "brick", None),
            P("shot", None, "brick", None),
            P(),
            P(),
            P(),
        ),
        out_specs=P("brick", "shot", None),
        check_vma=False,
    )
```

time: 300 us -> 148 us (0.49)
  waiting for transfers between devices: 189 us -> 0 us
  Pallas kernels: 0 us -> 139 us
  other arithmetic: 40.1 us -> 1.51 us
  matrix products: 22.3 us -> 0 us
  local copies, waits for them, and re-layouts: 26.6 us -> 5.62 us
  between operations: 14.2 us -> 1.34 us
  starting transfers between devices: 7.11 us -> 0 us
    all_gather x1 -> x0, waiting for transfers between devices: 150 us -> none  [per_device(): lax.all_gather(blocks[None], 'shot', axis=0, tiled=True)]
    pallas_call x0 -> x1, Pallas kernels: none -> 139 us  [per_device(): pl.pallas_call(functools.partial(kernel, shots, bricks, per_dev, chunks),...]
    ppermute x2 -> x0, waiting for transfers between devices: 39.7 us -> none  [the longest x1 24.4 us: extended(): after = lax.ppermute(first, axis, down)]
    add x2 -> x0, other arithmetic: 23.1 us -> none  [the longest x1 23.1 us: per_device(): updated = apply_inverse(forcing + neighbours, inv_re, inv_im)]
    dot_general x1 -> x0, matrix products: 22.3 us -> none  [per_device(): jnp.einsum('qkb,kbc->qc', weights, lax.all_gather(blocks[None], 'shot', a...]
    unnamed x27 -> x4, local copies, waits for them, and re-layouts: 13.9 us -> 0.01 us
    mul x5 -> x1, other arithmetic: 10.4 us -> 0.67 us  [per_device(): taper_xz = taper_x[:, None] * sine_taper(wide_z, float(wide_z))[None, :]]
    ppermute x2 -> x0, starting transfers between devices: 7.11 us -> none  [the longest x1 5.83 us: extended(): before = lax.ppermute(last, axis, up)]
  transfers between devices with their start and end apart: 3 -> 0, of which waited for: 3 -> 0; matrix products, arithmetic and copies ran while one was open for 2% -> 0% of each run, Pallas kernels for 0% -> 0%
where the time goes in v1:
time: 148 us; the launch traced here: 147 us
  Pallas kernels  139 us (94%)
  local copies, waits for them, and re-layouts  5.62 us (4%)
  other arithmetic  1.51 us (1%)
    pallas_call x1, Pallas kernels, per_device(): pl.pallas_call(functools.partial(kernel, shots, bricks, per_dev, chunks),...  139 us

profile of v1, /device:TPU:0, one launch (start us, length us, event | category | flops | bytes accessed | tf_op | source)
XLA Modules:
  0.0 147.3 jit_solution(9058382612260386595)
XLA Ops:
  0.0 0.0 copy-start
  0.0 1.2 dynamic_slice.4
  2.7 0.0 copy-start.1
  2.7 0.7 compare_select_fusion
  3.4 0.1 reshape.89
  3.5 0.0 copy-done
  3.5 0.8 gather_fusion
  4.3 0.1 reshape.88
  4.3 0.7 broadcast_multiply_fusion.txz_ref
  5.0 0.7 reshape.86.wt_ref
  5.7 0.0 copy-done.1
  5.7 138.8 %shard_map.55 = f32[4,2,8,2,8,256]{5,4,3,2,1,0:T(8,128)} custom-call(f32[1]{0:T(128)} %bitcast.1.mask_ref, f32[256]{0:T(256)} %copy-done.1, f32[2048]{0:T(1024)} %reshape.86.wt_ref, f32[8,256]{1,0:T(8,128)} %broadcast_multiply_fusion.txz_ref, f32[4,16,8,2,8,256]{5,4,3,2,1,0:T(8,128)} %bitcast.8, f32[16,8,2,8,256]{4,3,2,1,0:T(8,128)} %bitcast.9), custom_call_target="tpu_custom_call" | custom-call | flops 104857600 | bytes 12582912 | tf_op jit(solution)/shard_map/pallas_call | solution.py:424
  144.6 2.7 %reshape.83 = f32[1,4,65536]{2,1,0:T(4,128)} reshape(f32[4,2,8,2,8,256]{5,4,3,2,1,0:T(8,128)} %shard_map.55) | data formatting | bytes 2097152 | tf_op jit(solution)/shard_map/reshape | solution.py:452
  (4 shorter events, 0.1 us)
Async XLA Ops:
  0.0 3.5 %copy-start = (s32[32]{0:T(128)S(1)}, s32[32]{0:T(128)}, u32[]{:S(2)}) copy-start(s32[32]{0:T(128)} %param.9) | copy-start | bytes 388
  2.7 3.1 %copy-start.1 = (f32[256]{0:T(256)}, f32[256]{0:T(256)S(1)}, u32[]{:S(2)}) copy-start(f32[256]{0:T(256)S(1)} %multiply_sine_fusion.ty_ref) | copy-start | bytes 3076

commit v2 on v1

--- a/solution.py
+++ b/solution.py
@@ -8,6 +8,7 @@
 from jax.sharding import PartitionSpec as P
 
 BLOCKS = 8
+WIDTH = 4
 ROWS = 2
 MESH = pl.DeviceIdType.MESH
 
@@ -123,15 +124,15 @@
             inv[0, pl.ds(y, ROWS)] = ire
             inv[1, pl.ds(y, ROWS)] = iim
             mre, mim = ire * mask, iim * mask
+            fields = []
             for p in range(2):
                 a, b = sbuf[slot, 2 * p, j], sbuf[slot, 2 * p + 1, j]
-                fre = a * mre - b * mim
-                fim = a * mim + b * mre
-                for c, f in ((2 * p, fre), (2 * p + 1, fim)):
-                    f1[c, pl.ds(y + 1, ROWS)] = f
-                    for r in range(ROWS):
-                        hs_dn[k, c, pl.ds(j * ROWS + r, 1), :] = f[r, 0:1, :]
-                        hs_up[k, c, pl.ds(j * ROWS + r, 1), :] = f[r, 7:8, :]
+                fields += [a * mre - b * mim, a * mim + b * mre]
+            for c, f in enumerate(fields):
+                f1[c, pl.ds(y + 1, ROWS)] = f
+                for r in range(ROWS):
+                    hs_dn[k, c, pl.ds(j * ROWS + r, 1), :] = f[r, 0:1, :]
+                    hs_up[k, c, pl.ds(j * ROWS + r, 1), :] = f[r, 7:8, :]
             return carry
 
         lax.fori_loop(0, both, rows, 0)
@@ -213,11 +214,19 @@
             device_id=(sib, brick), device_id_type=MESH)
 
     def weighted(buf, k, r, source_pair):
-        start = (r * shots + 2 * source_pair) * BLOCKS
-        total = wt_ref[start] * buf[k, 0]
+        starts = [((r + i) * shots + 2 * source_pair) * BLOCKS for i in range(WIDTH)]
+        block = buf[k, 0]
+        totals = [wt_ref[start] * block for start in starts]
         for q in range(1, both):
-            total += wt_ref[start + q] * buf[k, q]
-        return total
+            block = buf[k, q]
+            totals = [total + wt_ref[start + q] * block for total, start in zip(totals, starts)]
+        return totals
+
+    def plus(totals, terms):
+        return [total + term for total, term in zip(totals, terms)]
+
+    def entries(buf, k, q):
+        return [buf[k, q + i] for i in range(WIDTH)]
 
     def produce(k):
         @pl.when(brick > 0)
@@ -232,20 +241,23 @@
                 src_ref=hs_dn.at[k], dst_ref=h_after.at[k], send_sem=dn_s.at[k], recv_sem=dn_r.at[k],
                 device_id=(shot, brick + 1), device_id_type=MESH).wait_recv()
 
-        def other(b, carry):
-            for r in range(ROWS):
-                gsend[k, b, r] = image(k, 2 * b + (1 - core), r)
+        def images(b, side):
+            return [(b + i, r, image(k, 2 * (b + i) + side, r)) for i in range(2) for r in range(ROWS)]
+
+        def other(step, carry):
+            for b, r, value in images(2 * step, 1 - core):
+                gsend[k, b, r] = value
             return carry
 
-        lax.fori_loop(0, BLOCKS, other, 0)
+        lax.fori_loop(0, BLOCKS // 2, other, 0)
         sib_copy(k).start()
 
-        def mine(b, carry):
-            for r in range(ROWS):
-                raw[k, core * BLOCKS + b, r] = image(k, 2 * b + core, r)
+        def mine(step, carry):
+            for b, r, value in images(2 * step, core):
+                raw[k, core * BLOCKS + b, r] = value
             return carry
 
-        lax.fori_loop(0, BLOCKS, mine, 0)
+        lax.fori_loop(0, BLOCKS // 2, mine, 0)
 
     def right_flow(k):
         for s in range(pairs - 1):
@@ -257,17 +269,19 @@
             @pl.when(pair == s)
             def _(s=s):
                 if s > 0:
-                    def body(q, carry):
+                    def body(step, carry):
+                        q = step * WIDTH
                         r = (s + 1) * group + q
-                        total = weighted(raw, k, r, s)
+                        totals = weighted(raw, k, r, s)
                         if s == 1:
-                            total += weighted(rin, k, r, 0)
+                            totals = plus(totals, weighted(rin, k, r, 0))
                         else:
-                            total += rin[k, q + group]
-                        rout[k, q] = total
+                            totals = plus(totals, entries(rin, k, q + group))
+                        for i in range(WIDTH):
+                            rout[k, q + i] = totals[i]
                         return carry
 
-                    lax.fori_loop(0, (pairs - 1 - s) * group, body, 0)
+                    lax.fori_loop(0, (pairs - 1 - s) * group // WIDTH, body, 0)
                 right_copy(k, s).start()
 
     def left_flow(k):
@@ -280,37 +294,41 @@
             @pl.when(pair == s)
             def _(s=s):
                 if s < pairs - 1:
-                    def body(q, carry):
-                        total = weighted(raw, k, q, s)
+                    def body(step, carry):
+                        q = step * WIDTH
+                        totals = weighted(raw, k, q, s)
                         if s == pairs - 2:
-                            total += weighted(lin, k, q, pairs - 1)
+                            totals = plus(totals, weighted(lin, k, q, pairs - 1))
                         else:
-                            total += lin[k, q]
-                        lout[k, q] = total
+                            totals = plus(totals, entries(lin, k, q))
+                        for i in range(WIDTH):
+                            lout[k, q + i] = totals[i]
                         return carry
 
-                    lax.fori_loop(0, s * group, body, 0)
+                    lax.fori_loop(0, s * group // WIDTH, body, 0)
                 left_copy(k, s).start()
 
     def finish(k):
         for s in range(pairs):
             @pl.when(pair == s)
             def _(s=s):
-                def body(q, carry):
+                def body(step, carry):
+                    q = step * WIDTH
                     r = s * group + q
-                    total = weighted(raw, k, r, s)
+                    totals = weighted(raw, k, r, s)
                     if s == 1:
-                        total += weighted(rin, k, r, 0)
+                        totals = plus(totals, weighted(rin, k, r, 0))
                     elif s > 1:
-                        total += rin[k, q]
+                        totals = plus(totals, entries(rin, k, q))
                     if s == pairs - 2:
-                        total += weighted(lin, k, r, pairs - 1)
+                        totals = plus(totals, weighted(lin, k, r, pairs - 1))
                     elif s < pairs - 1:
-                        total += lin[k, s * group + q]
-                    own[k, q] = total
+                        totals = plus(totals, entries(lin, k, s * group + q))
+                    for i in range(WIDTH):
+                        own[k, q + i] = totals[i]
                     return carry
 
-                lax.fori_loop(0, group, body, 0)
+                lax.fori_loop(0, group // WIDTH, body, 0)
 
         fin_copy(k).start()
         for q in range(per_dev):

time: 148 us -> 144 us (0.973)
  Pallas kernels: 139 us -> 135 us
    pallas_call x1, Pallas kernels: 139 us -> 135 us  [per_device(): pl.pallas_call(functools.partial(kernel, shots, bricks, per_dev, chunks),...]
where the time goes in v2:
time: 144 us; the launch traced here: 143 us
  Pallas kernels  135 us (94%)
  local copies, waits for them, and re-layouts  5.62 us (4%)
  other arithmetic  1.51 us (1%)
    pallas_call x1, Pallas kernels, per_device(): pl.pallas_call(functools.partial(kernel, shots, bricks, per_dev, chunks),...  135 us

profile of v2, /device:TPU:0, one launch (start us, length us, event | category | flops | bytes accessed | tf_op | source)
XLA Modules:
  0.0 143.1 jit_solution(3085741419609046770)
XLA Ops:
  0.0 0.0 copy-start
  0.0 1.2 dynamic_slice.4
  2.7 0.0 copy-start.1
  2.7 0.7 compare_select_fusion
  3.4 0.1 reshape.89
  3.5 0.0 copy-done
  3.5 0.8 gather_fusion
  4.3 0.1 reshape.88
  4.3 0.7 broadcast_multiply_fusion.txz_ref
  5.0 0.7 reshape.86.wt_ref
  5.7 0.0 copy-done.1
  5.7 134.7 %shard_map.55 = f32[4,2,8,2,8,256]{5,4,3,2,1,0:T(8,128)} custom-call(f32[1]{0:T(128)} %bitcast.1.mask_ref, f32[256]{0:T(256)} %copy-done.1, f32[2048]{0:T(1024)} %reshape.86.wt_ref, f32[8,256]{1,0:T(8,128)} %broadcast_multiply_fusion.txz_ref, f32[4,16,8,2,8,256]{5,4,3,2,1,0:T(8,128)} %bitcast.8, f32[16,8,2,8,256]{4,3,2,1,0:T(8,128)} %bitcast.9), custom_call_target="tpu_custom_call" | custom-call | flops 104857600 | bytes 12582912 | tf_op jit(solution)/shard_map/pallas_call | solution.py:442
  140.4 2.7 %reshape.83 = f32[1,4,65536]{2,1,0:T(4,128)} reshape(f32[4,2,8,2,8,256]{5,4,3,2,1,0:T(8,128)} %shard_map.55) | data formatting | bytes 2097152 | tf_op jit(solution)/shard_map/reshape | solution.py:470
  (4 shorter events, 0.1 us)
Async XLA Ops:
  0.0 3.5 %copy-start = (s32[32]{0:T(128)S(1)}, s32[32]{0:T(128)}, u32[]{:S(2)}) copy-start(s32[32]{0:T(128)} %param.9) | copy-start | bytes 388
  2.7 3.1 %copy-start.1 = (f32[256]{0:T(256)}, f32[256]{0:T(256)S(1)}, u32[]{:S(2)}) copy-start(f32[256]{0:T(256)S(1)} %multiply_sine_fusion.ty_ref) | copy-start | bytes 3076

commit v3 on v2

--- a/solution.py
+++ b/solution.py
@@ -8,8 +8,8 @@
 from jax.sharding import PartitionSpec as P
 
 BLOCKS = 8
-WIDTH = 4
-ROWS = 2
+WIDTH = 8
+ROWS = 1
 MESH = pl.DeviceIdType.MESH
 
 shift_beta = 0.5
@@ -242,22 +242,22 @@
                 device_id=(shot, brick + 1), device_id_type=MESH).wait_recv()
 
         def images(b, side):
-            return [(b + i, r, image(k, 2 * (b + i) + side, r)) for i in range(2) for r in range(ROWS)]
+            return [(b + i, r, image(k, 2 * (b + i) + side, r)) for i in range(4) for r in range(ROWS)]
 
         def other(step, carry):
-            for b, r, value in images(2 * step, 1 - core):
+            for b, r, value in images(4 * step, 1 - core):
                 gsend[k, b, r] = value
             return carry
 
-        lax.fori_loop(0, BLOCKS // 2, other, 0)
+        lax.fori_loop(0, BLOCKS // 4, other, 0)
         sib_copy(k).start()
 
         def mine(step, carry):
-            for b, r, value in images(2 * step, core):
+            for b, r, value in images(4 * step, core):
                 raw[k, core * BLOCKS + b, r] = value
             return carry
 
-        lax.fori_loop(0, BLOCKS // 2, mine, 0)
+        lax.fori_loop(0, BLOCKS // 4, mine, 0)
 
     def right_flow(k):
         for s in range(pairs - 1):

time: 144 us -> 190 us (1.32)
  Pallas kernels: 135 us -> 181 us
    pallas_call x1, Pallas kernels: 135 us -> 181 us  [per_device(): pl.pallas_call(functools.partial(kernel, shots, bricks, per_dev, chunks),...]
where the time goes in v3:
time: 190 us
  Pallas kernels  181 us (95%)
  local copies, waits for them, and re-layouts  5.62 us (3%)
    pallas_call x1, Pallas kernels, per_device(): pl.pallas_call(functools.partial(kernel, shots, bricks, per_dev, chunks),...  181 us

profile of v3, /device:TPU:0, one launch (start us, length us, event | category | flops | bytes accessed | tf_op | source)
XLA Modules:
  0.0 189.8 jit_solution(15070538149699790290)
XLA Ops:
  0.0 0.0 copy-start
  0.0 1.2 dynamic_slice.4
  2.7 0.0 copy-start.1
  2.7 0.7 compare_select_fusion
  3.4 0.1 reshape.89
  3.5 0.0 copy-done
  3.5 0.8 gather_fusion
  4.3 0.1 reshape.88
  4.3 0.7 broadcast_multiply_fusion.txz_ref
  5.0 0.7 reshape.86.wt_ref
  5.7 0.0 copy-done.1
  5.7 181.4 %shard_map.55 = f32[4,2,16,1,8,256]{5,4,3,2,1,0:T(8,128)} custom-call(f32[1]{0:T(128)} %bitcast.1.mask_ref, f32[256]{0:T(256)} %copy-done.1, f32[2048]{0:T(1024)} %reshape.86.wt_ref, f32[8,256]{1,0:T(8,128)} %broadcast_multiply_fusion.txz_ref, f32[4,16,16,1,8,256]{5,4,3,2,1,0:T(8,128)} %bitcast.8, f32[16,16,1,8,256]{4,3,2,1,0:T(8,128)} %bitcast.9), custom_call_target="tpu_custom_call" | custom-call | flops 104857600 | bytes 12582912 | tf_op jit(solution)/shard_map/pallas_call | solution.py:442
  187.1 2.7 %reshape.83 = f32[1,4,65536]{2,1,0:T(4,128)} reshape(f32[4,2,16,1,8,256]{5,4,3,2,1,0:T(8,128)} %shard_map.55) | data formatting | bytes 2097152 | tf_op jit(solution)/shard_map/reshape | solution.py:470
  (4 shorter events, 0.1 us)
Async XLA Ops:
  0.0 3.5 %copy-start = (s32[32]{0:T(128)S(1)}, s32[32]{0:T(128)}, u32[]{:S(2)}) copy-start(s32[32]{0:T(128)} %param.9) | copy-start | bytes 388
  2.7 3.1 %copy-start.1 = (f32[256]{0:T(256)}, f32[256]{0:T(256)S(1)}, u32[]{:S(2)}) copy-start(f32[256]{0:T(256)S(1)} %multiply_sine_fusion.ty_ref) | copy-start | bytes 3076

commit v4 on v3

--- a/solution.py
+++ b/solution.py
@@ -8,8 +8,8 @@
 from jax.sharding import PartitionSpec as P
 
 BLOCKS = 8
-WIDTH = 8
-ROWS = 1
+WIDTH = 2
+ROWS = 4
 MESH = pl.DeviceIdType.MESH
 
 shift_beta = 0.5
@@ -242,22 +242,22 @@
                 device_id=(shot, brick + 1), device_id_type=MESH).wait_recv()
 
         def images(b, side):
-            return [(b + i, r, image(k, 2 * (b + i) + side, r)) for i in range(4) for r in range(ROWS)]
+            return [(b + i, r, image(k, 2 * (b + i) + side, r)) for i in range(1) for r in range(ROWS)]
 
         def other(step, carry):
-            for b, r, value in images(4 * step, 1 - core):
+            for b, r, value in images(step, 1 - core):
                 gsend[k, b, r] = value
             return carry
 
-        lax.fori_loop(0, BLOCKS // 4, other, 0)
+        lax.fori_loop(0, BLOCKS, other, 0)
         sib_copy(k).start()
 
         def mine(step, carry):
-            for b, r, value in images(4 * step, core):
+            for b, r, value in images(step, core):
                 raw[k, core * BLOCKS + b, r] = value
             return carry
 
-        lax.fori_loop(0, BLOCKS // 4, mine, 0)
+        lax.fori_loop(0, BLOCKS, mine, 0)
 
     def right_flow(k):
         for s in range(pairs - 1):

time: 190 us -> 133 us (0.70)
  Pallas kernels: 181 us -> 124 us
    pallas_call x1, Pallas kernels: 181 us -> 124 us  [per_device(): pl.pallas_call(functools.partial(kernel, shots, bricks, per_dev, chunks),...]
where the time goes in v4:
time: 133 us; the launch traced here: 132 us
  Pallas kernels  124 us (93%)
  local copies, waits for them, and re-layouts  5.62 us (4%)
  other arithmetic  1.51 us (1%)
  between operations  1.34 us (1%)
    pallas_call x1, Pallas kernels, per_device(): pl.pallas_call(functools.partial(kernel, shots, bricks, per_dev, chunks),...  124 us
    reshape x1, local copies, waits for them, and re-layouts, per_device(): return out.reshape(1, per_dev, -1)  2.72 us

profile of v4, /device:TPU:0, one launch (start us, length us, event | category | flops | bytes accessed | tf_op | source)
XLA Modules:
  0.0 132.5 jit_solution(11042739043719125250)
XLA Ops:
  0.0 0.0 copy-start
  0.0 1.2 dynamic_slice.4
  2.7 0.0 copy-start.1
  2.7 0.7 compare_select_fusion
  3.4 0.1 reshape.89
  3.5 0.0 copy-done
  3.5 0.8 gather_fusion
  4.3 0.1 reshape.88
  4.3 0.7 broadcast_multiply_fusion.txz_ref
  5.0 0.7 reshape.86.wt_ref
  5.7 0.0 copy-done.1
  5.7 124.0 %shard_map.55 = f32[4,2,4,4,8,256]{5,4,3,2,1,0:T(8,128)} custom-call(f32[1]{0:T(128)} %bitcast.1.mask_ref, f32[256]{0:T(256)} %copy-done.1, f32[2048]{0:T(1024)} %reshape.86.wt_ref, f32[8,256]{1,0:T(8,128)} %broadcast_multiply_fusion.txz_ref, f32[4,16,4,4,8,256]{5,4,3,2,1,0:T(8,128)} %bitcast.8, f32[16,4,4,8,256]{4,3,2,1,0:T(8,128)} %bitcast.9), custom_call_target="tpu_custom_call" | custom-call | flops 104857600 | bytes 12582912 | tf_op jit(solution)/shard_map/pallas_call | solution.py:442
  129.8 2.7 %reshape.83 = f32[1,4,65536]{2,1,0:T(4,128)} reshape(f32[4,2,4,4,8,256]{5,4,3,2,1,0:T(8,128)} %shard_map.55) | data formatting | bytes 2097152 | tf_op jit(solution)/shard_map/reshape | solution.py:470
  (4 shorter events, 0.1 us)
Async XLA Ops:
  0.0 3.5 %copy-start = (s32[32]{0:T(128)S(1)}, s32[32]{0:T(128)}, u32[]{:S(2)}) copy-start(s32[32]{0:T(128)} %param.9) | copy-start | bytes 388
  2.7 3.1 %copy-start.1 = (f32[256]{0:T(256)}, f32[256]{0:T(256)S(1)}, u32[]{:S(2)}) copy-start(f32[256]{0:T(256)S(1)} %multiply_sine_fusion.ty_ref) | copy-start | bytes 3076

commit v5 on v4

--- a/solution.py
+++ b/solution.py
@@ -334,7 +334,9 @@
         for q in range(per_dev):
             out_ref[q, core, k] = own[k, core * per_dev + q]
 
-    near_lag, far_lag, end_lag = 1, 2, 3
+    at_end = (pair == 0) | (pair == pairs - 1)
+    near_lag = jnp.where(at_end, 1, 2)
+    far_lag, end_lag = 3, 4
     is_left = pair < pairs // 2
     right_lag = jnp.where(is_left, near_lag, far_lag)
     left_lag = jnp.where(is_left, far_lag, near_lag)

time: 133 us -> 114 us (0.86)
  Pallas kernels: 124 us -> 105 us
    pallas_call x1, Pallas kernels: 124 us -> 105 us  [per_device(): pl.pallas_call(functools.partial(kernel, shots, bricks, per_dev, chunks),...]
where the time goes in v5:
time: 114 us
  Pallas kernels  105 us (92%)
  local copies, waits for them, and re-layouts  5.62 us (5%)
  other arithmetic  1.51 us (1%)
  between operations  1.34 us (1%)
    pallas_call x1, Pallas kernels, per_device(): pl.pallas_call(functools.partial(kernel, shots, bricks, per_dev, chunks),...  105 us
    reshape x1, local copies, waits for them, and re-layouts, per_device(): return out.reshape(1, per_dev, -1)  2.72 us

profile of v5, /device:TPU:0, one launch (start us, length us, event | category | flops | bytes accessed | tf_op | source)
XLA Modules:
  0.0 113.8 jit_solution(13415476177480779328)
XLA Ops:
  0.0 0.0 copy-start
  0.0 1.2 %dynamic_slice.4 = s32[1]{0:T(128)} dynamic-slice(s32[8]{0:T(128)} %param.7, s32[]{:T(128)S(6)} %select_n.22), dynamic_slice_sizes={1} | dynamic-slice | bytes 12 | tf_op jit(solution)/shard_map/dynamic_slice | solution.py:421
  2.7 0.0 copy-start.1
  2.7 0.7 compare_select_fusion
  3.4 0.1 reshape.89
  3.5 0.0 copy-done
  3.5 0.8 gather_fusion
  4.3 0.1 reshape.88
  4.3 0.7 broadcast_multiply_fusion.txz_ref
  5.0 0.7 reshape.86.wt_ref
  5.7 0.0 copy-done.1
  5.7 105.3 %shard_map.55 = f32[4,2,4,4,8,256]{5,4,3,2,1,0:T(8,128)} custom-call(f32[1]{0:T(128)} %bitcast.1.mask_ref, f32[256]{0:T(256)} %copy-done.1, f32[2048]{0:T(1024)} %reshape.86.wt_ref, f32[8,256]{1,0:T(8,128)} %broadcast_multiply_fusion.txz_ref, f32[4,16,4,4,8,256]{5,4,3,2,1,0:T(8,128)} %bitcast.8, f32[16,4,4,8,256]{4,3,2,1,0:T(8,128)} %bitcast.9), custom_call_target="tpu_custom_call" | custom-call | flops 104857600 | bytes 12582912 | tf_op jit(solution)/shard_map/pallas_call | solution.py:444
  111.1 2.7 %reshape.83 = f32[1,4,65536]{2,1,0:T(4,128)} reshape(f32[4,2,4,4,8,256]{5,4,3,2,1,0:T(8,128)} %shard_map.55) | data formatting | bytes 2097152 | tf_op jit(solution)/shard_map/reshape | solution.py:472
  (4 shorter events, 0.1 us)
Async XLA Ops:
  0.0 3.5 %copy-start = (s32[32]{0:T(128)S(1)}, s32[32]{0:T(128)}, u32[]{:S(2)}) copy-start(s32[32]{0:T(128)} %param.9) | copy-start | bytes 388
  2.7 3.1 %copy-start.1 = (f32[256]{0:T(256)}, f32[256]{0:T(256)S(1)}, u32[]{:S(2)}) copy-start(f32[256]{0:T(256)S(1)} %multiply_sine_fusion.ty_ref) | copy-start | bytes 3076
